TPU v7x, 32 devices: a whole 2x2x4 slice. The times are simulated.
32 devices in a mesh: px: 8 (over y, x, core), py: 4 (over z).
Axes of the slice: x: 2, y: 2, z: 4, core: 2. Of those that a mesh axis runs over, the one named last changes fastest.
Arguments:
- start_vecs: float32 [512, 64, 128], P(('px', 'py')), may hold values from -6 to 6
- local_tiles: bfloat16 [512, 4, 128, 128], P(('px', 'py')), may hold values from -0.078125 to 0.078125
- local_cols: int32 [512, 4], P(('px', 'py')), may hold values from 0 to 15
- halo_tiles: bfloat16 [512, 128, 128], P(('px', 'py')), may hold values from -0.078125 to 0.078125
- halo_slot: int32 [512], P(('px', 'py')), may hold values from 0 to 7
- boundary: int32 [128, 2], P(('px', 'py')), may hold values from 0 to 15
Outputs:
- filtered: float32 [512, 64, 128], P(('px', 'py'))
- gram_matrix: float32 [64, 64], replicated
Inputs may be any that keep to these rules, and one draw needn't show every extreme that they name: `local_cols`: local block indices within the partition. `boundary`: local block indices within the partition.
All inputs are finite; a program needn't handle non-finite values.
Results may differ from a plain program's by a relative error of at most 0.0055.
Values may be sent and summed in bfloat16 or wider, within the bound.
A program may use at most 64 MiB of HBM per device.

v0:
```python
import jax
import jax.numpy as jnp
from jax import lax
from jax.sharding import PartitionSpec as P

DEG = 9


def from_behind(value, axis, steps):
    count = lax.axis_size(axis)
    pairs = [(source, (source + steps) % count) for source in range(count)]
    return lax.ppermute(value, axis, pairs)


def operator_apply(current, local_tiles, local_cols, halo_tiles, halo_slot, boundary):
    rounded = current.astype(jnp.bfloat16)
    outgoing = rounded[boundary]
    from_xlow = from_behind(outgoing[0], "px", 1)
    from_xhigh = from_behind(outgoing[1], "px", -1)
    from_ylow = from_behind(outgoing[2], "py", 1)
    from_yhigh = from_behind(outgoing[3], "py", -1)
    received = jnp.concatenate([from_xlow, from_xhigh, from_ylow, from_yhigh], axis=0)
    gathered = rounded[local_cols]
    product = jnp.einsum(
        "rtkj,rtij->rki", gathered, local_tiles, preferred_element_type=jnp.float32
    )
    coupled = jnp.einsum(
        "rkj,rij->rki", received[halo_slot], halo_tiles, preferred_element_type=jnp.float32
    )
    return product + coupled


def shards(start_vecs, local_tiles, local_cols, halo_tiles, halo_slot, boundary):

    def step_apply(current):
        return operator_apply(current, local_tiles, local_cols, halo_tiles, halo_slot, boundary)

    first_vecs = step_apply(start_vecs)

    def advance(step_index, state_pair):
        older_vec, newer_vec = state_pair
        return (newer_vec, 2.0 * step_apply(newer_vec) - older_vec)

    previous, current = lax.fori_loop(0, DEG - 1, advance, (start_vecs, first_vecs))
    total_rows = current.shape[0] * current.shape[2] * lax.axis_size("px") * lax.axis_size("py")
    squares = lax.psum(jnp.sum(current * current, axis=(0, 2)), ("px", "py"))
    scales = lax.rsqrt(squares / total_rows + 1e-06)
    filtered = current * scales[None, :, None]
    partial_gram = jnp.einsum("rkj,rlj->kl", filtered, filtered, precision=lax.Precision.HIGHEST)
    gram_matrix = lax.psum(partial_gram, ("px", "py")) / total_rows
    return (filtered, gram_matrix)


def solution(mesh):
    return jax.shard_map(
        shards,
        mesh=mesh,
        in_specs=(
            P(("px", "py"), None, None),
            P(("px", "py"), None, None, None),
            P(("px", "py"), None),
            P(("px", "py"), None, None),
            P(("px", "py")),
            P(("px", "py"), None),
        ),
        out_specs=(P(("px", "py"), None, None), P()),
        check_vma=False,
    )
```

profile of v0, /device:TPU:0, one launch (start us, length us, event | category | flops | bytes accessed | tf_op | source)
XLA Modules:
  0.0 208.9 jit_solution(8709277243146897186)
XLA Ops:
  3.9 2.6 %collective-permute-start.6 = (bf16[2,64,128]{2,1,0:T(8,128)(2,1)S(1)}, bf16[2,64,128]{2,1,0:T(8,128)(2,1)S(1)}, u32[]{:S(2)}, u32[]{:S(2)}) collective-permute-start(bf16[2,64,128]{2,1,0:T(8,128)(2,1)S(1)} %get-tuple-element.66), channel_id=1, source_target_pairs={{0,1},{1,2},{2,3},{3,0},{4,5},{5,6},{6,7},{7,4},{8,9},{9,10},{10,1... | collective-permute-start | bytes 98312 | tf_op jit(solution)/shard_map/ppermute | solution.py:12
  6.5 2.3 %collective-permute-start.5 = (bf16[2,64,128]{2,1,0:T(8,128)(2,1)S(1)}, bf16[2,64,128]{2,1,0:T(8,128)(2,1)S(1)}, u32[]{:S(2)}, u32[]{:S(2)}) collective-permute-start(bf16[2,64,128]{2,1,0:T(8,128)(2,1)S(1)} %get-tuple-element.67), channel_id=1, source_target_pairs={{0,28},{4,0},{8,4},{12,8},{16,12},{20,16},{24,20},{28,24},{1,29},{... | collective-permute-start | bytes 98312 | tf_op jit(solution)/shard_map/ppermute | solution.py:12
  8.8 2.3 %collective-permute-start.7 = (bf16[2,64,128]{2,1,0:T(8,128)(2,1)S(1)}, bf16[2,64,128]{2,1,0:T(8,128)(2,1)S(1)}, u32[]{:S(2)}, u32[]{:S(2)}) collective-permute-start(bf16[2,64,128]{2,1,0:T(8,128)(2,1)S(1)} %get-tuple-element.68), channel_id=1, source_target_pairs={{0,3},{1,0},{2,1},{3,2},{4,7},{5,4},{6,5},{7,6},{8,11},{9,8},{10,9... | collective-permute-start | bytes 98312 | tf_op jit(solution)/shard_map/ppermute | solution.py:12
  13.0 2.9 %convolution_bitcast_fusion.1 = f32[16,64,128]{2,1,0:T(8,128)} fusion(bf16[16,4,64,128]{3,2,1,0:T(8,128)(2,1)} %bitcast.53, bf16[16,4,128,128]{3,2,1,0:T(8,128)(2,1)S(1)} %copy-done), kind=kOutput, calls=%fused_computation.18 | convolution fusion | flops 134217728 | bytes 3670016 | tf_op jit(solution)/shard_map/rtkj,rtij->rki/dot_general | solution.py:24
  18.1 108.5 %while.12 = (s32[]{:T(128)}, f32[16,64,128]{2,1,0:T(8,128)}, f32[16,64,128]{2,1,0:T(8,128)S(1)}, s32[16,4]{0,1:T(4,128)S(1)}, bf16[16,4,128,128]{3,2,1,0:T(8,128...) while((s32[]{:T(128)}, f32[16,64,128]{2,1,0:T(8,128)}, ...), condition=%wide.region_1.0_spmd, body=%wide.region_0.0_spmd.sunk | while | flops 168496400 | bytes 23345988 | solution.py:44
  22.5 2.4 %convolution_bitcast_fusion.4 = f32[16,64,128]{2,1,0:T(8,128)S(1)} fusion(bf16[16,4,64,128]{3,2,1,0:T(8,128)(2,1)S(1)} %bitcast.52, bf16[16,4,128,128]{3,2,1,0:T(8,128)(2,1)} %get-tuple-element.162), kind=kOutput, calls=%fused_computation.6.clone.1 | convolution fusion | flops 134217728 | bytes 3670016 | tf_op jit(solution)/shard_map/while/body/eval_jaxpr/rtkj,rtij->rki/dot_general | solution.py:24
  31.1 2.4 %collective-permute-start = (bf16[2,64,128]{2,1,0:T(8,128)(2,1)S(1)}, bf16[2,64,128]{2,1,0:T(8,128)(2,1)S(1)}, u32[]{:S(2)}, u32[]{:S(2)}) collective-permute-start(bf16[2,64,128]{2,1,0:T(8,128)(2,1)S(1)} %get-tuple-element.122), channel_id=1, source_target_pairs={{0,3},{1,0},{2,1},{3,2},{4,7},{5,4},{6,5},{7,6},{8,11},{9,8},{10,9... | collective-permute-start | bytes 98312 | tf_op jit(solution)/shard_map/while/body/eval_jaxpr/ppermute | solution.py:12
  36.0 2.4 %convolution_bitcast_fusion.4 = f32[16,64,128]{2,1,0:T(8,128)S(1)} fusion(bf16[16,4,64,128]{3,2,1,0:T(8,128)(2,1)S(1)} %bitcast.52, bf16[16,4,128,128]{3,2,1,0:T(8,128)(2,1)} %get-tuple-element.162), kind=kOutput, calls=%fused_computation.6.clone.1 | convolution fusion | flops 134217728 | bytes 3670016 | tf_op jit(solution)/shard_map/while/body/eval_jaxpr/rtkj,rtij->rki/dot_general | solution.py:24
  43.8 3.6 %collective-permute-start = (bf16[2,64,128]{2,1,0:T(8,128)(2,1)S(1)}, bf16[2,64,128]{2,1,0:T(8,128)(2,1)S(1)}, u32[]{:S(2)}, u32[]{:S(2)}) collective-permute-start(bf16[2,64,128]{2,1,0:T(8,128)(2,1)S(1)} %get-tuple-element.122), channel_id=1, source_target_pairs={{0,3},{1,0},{2,1},{3,2},{4,7},{5,4},{6,5},{7,6},{8,11},{9,8},{10,9... | collective-permute-start | bytes 98312 | tf_op jit(solution)/shard_map/while/body/eval_jaxpr/ppermute | solution.py:12
  49.9 2.4 %convolution_bitcast_fusion.4 = f32[16,64,128]{2,1,0:T(8,128)S(1)} fusion(bf16[16,4,64,128]{3,2,1,0:T(8,128)(2,1)S(1)} %bitcast.52, bf16[16,4,128,128]{3,2,1,0:T(8,128)(2,1)} %get-tuple-element.162), kind=kOutput, calls=%fused_computation.6.clone.1 | convolution fusion | flops 134217728 | bytes 3670016 | tf_op jit(solution)/shard_map/while/body/eval_jaxpr/rtkj,rtij->rki/dot_general | solution.py:24
  57.8 3.6 %collective-permute-start = (bf16[2,64,128]{2,1,0:T(8,128)(2,1)S(1)}, bf16[2,64,128]{2,1,0:T(8,128)(2,1)S(1)}, u32[]{:S(2)}, u32[]{:S(2)}) collective-permute-start(bf16[2,64,128]{2,1,0:T(8,128)(2,1)S(1)} %get-tuple-element.122), channel_id=1, source_target_pairs={{0,3},{1,0},{2,1},{3,2},{4,7},{5,4},{6,5},{7,6},{8,11},{9,8},{10,9... | collective-permute-start | bytes 98312 | tf_op jit(solution)/shard_map/while/body/eval_jaxpr/ppermute | solution.py:12
  63.9 2.4 %convolution_bitcast_fusion.4 = f32[16,64,128]{2,1,0:T(8,128)S(1)} fusion(bf16[16,4,64,128]{3,2,1,0:T(8,128)(2,1)S(1)} %bitcast.52, bf16[16,4,128,128]{3,2,1,0:T(8,128)(2,1)} %get-tuple-element.162), kind=kOutput, calls=%fused_computation.6.clone.1 | convolution fusion | flops 134217728 | bytes 3670016 | tf_op jit(solution)/shard_map/while/body/eval_jaxpr/rtkj,rtij->rki/dot_general | solution.py:24
  71.7 3.6 %collective-permute-start = (bf16[2,64,128]{2,1,0:T(8,128)(2,1)S(1)}, bf16[2,64,128]{2,1,0:T(8,128)(2,1)S(1)}, u32[]{:S(2)}, u32[]{:S(2)}) collective-permute-start(bf16[2,64,128]{2,1,0:T(8,128)(2,1)S(1)} %get-tuple-element.122), channel_id=1, source_target_pairs={{0,3},{1,0},{2,1},{3,2},{4,7},{5,4},{6,5},{7,6},{8,11},{9,8},{10,9... | collective-permute-start | bytes 98312 | tf_op jit(solution)/shard_map/while/body/eval_jaxpr/ppermute | solution.py:12
  77.8 2.4 %convolution_bitcast_fusion.4 = f32[16,64,128]{2,1,0:T(8,128)S(1)} fusion(bf16[16,4,64,128]{3,2,1,0:T(8,128)(2,1)S(1)} %bitcast.52, bf16[16,4,128,128]{3,2,1,0:T(8,128)(2,1)} %get-tuple-element.162), kind=kOutput, calls=%fused_computation.6.clone.1 | convolution fusion | flops 134217728 | bytes 3670016 | tf_op jit(solution)/shard_map/while/body/eval_jaxpr/rtkj,rtij->rki/dot_general | solution.py:24
  85.7 3.6 %collective-permute-start = (bf16[2,64,128]{2,1,0:T(8,128)(2,1)S(1)}, bf16[2,64,128]{2,1,0:T(8,128)(2,1)S(1)}, u32[]{:S(2)}, u32[]{:S(2)}) collective-permute-start(bf16[2,64,128]{2,1,0:T(8,128)(2,1)S(1)} %get-tuple-element.122), channel_id=1, source_target_pairs={{0,3},{1,0},{2,1},{3,2},{4,7},{5,4},{6,5},{7,6},{8,11},{9,8},{10,9... | collective-permute-start | bytes 98312 | tf_op jit(solution)/shard_map/while/body/eval_jaxpr/ppermute | solution.py:12
  91.8 2.4 %convolution_bitcast_fusion.4 = f32[16,64,128]{2,1,0:T(8,128)S(1)} fusion(bf16[16,4,64,128]{3,2,1,0:T(8,128)(2,1)S(1)} %bitcast.52, bf16[16,4,128,128]{3,2,1,0:T(8,128)(2,1)} %get-tuple-element.162), kind=kOutput, calls=%fused_computation.6.clone.1 | convolution fusion | flops 134217728 | bytes 3670016 | tf_op jit(solution)/shard_map/while/body/eval_jaxpr/rtkj,rtij->rki/dot_general | solution.py:24
  95.7 1.8 fusion.28
  99.6 3.6 %collective-permute-start = (bf16[2,64,128]{2,1,0:T(8,128)(2,1)S(1)}, bf16[2,64,128]{2,1,0:T(8,128)(2,1)S(1)}, u32[]{:S(2)}, u32[]{:S(2)}) collective-permute-start(bf16[2,64,128]{2,1,0:T(8,128)(2,1)S(1)} %get-tuple-element.122), channel_id=1, source_target_pairs={{0,3},{1,0},{2,1},{3,2},{4,7},{5,4},{6,5},{7,6},{8,11},{9,8},{10,9... | collective-permute-start | bytes 98312 | tf_op jit(solution)/shard_map/while/body/eval_jaxpr/ppermute | solution.py:12
  105.7 2.4 %convolution_bitcast_fusion.4 = f32[16,64,128]{2,1,0:T(8,128)S(1)} fusion(bf16[16,4,64,128]{3,2,1,0:T(8,128)(2,1)S(1)} %bitcast.52, bf16[16,4,128,128]{3,2,1,0:T(8,128)(2,1)} %get-tuple-element.162), kind=kOutput, calls=%fused_computation.6.clone.1 | convolution fusion | flops 134217728 | bytes 3670016 | tf_op jit(solution)/shard_map/while/body/eval_jaxpr/rtkj,rtij->rki/dot_general | solution.py:24
  109.7 1.8 fusion.28
  113.6 3.6 %collective-permute-start = (bf16[2,64,128]{2,1,0:T(8,128)(2,1)S(1)}, bf16[2,64,128]{2,1,0:T(8,128)(2,1)S(1)}, u32[]{:S(2)}, u32[]{:S(2)}) collective-permute-start(bf16[2,64,128]{2,1,0:T(8,128)(2,1)S(1)} %get-tuple-element.122), channel_id=1, source_target_pairs={{0,3},{1,0},{2,1},{3,2},{4,7},{5,4},{6,5},{7,6},{8,11},{9,8},{10,9... | collective-permute-start | bytes 98312 | tf_op jit(solution)/shard_map/while/body/eval_jaxpr/ppermute | solution.py:12
  119.7 2.4 %convolution_bitcast_fusion.4 = f32[16,64,128]{2,1,0:T(8,128)S(1)} fusion(bf16[16,4,64,128]{3,2,1,0:T(8,128)(2,1)S(1)} %bitcast.52, bf16[16,4,128,128]{3,2,1,0:T(8,128)(2,1)} %get-tuple-element.162), kind=kOutput, calls=%fused_computation.6.clone.1 | convolution fusion | flops 134217728 | bytes 3670016 | tf_op jit(solution)/shard_map/while/body/eval_jaxpr/rtkj,rtij->rki/dot_general | solution.py:24
  126.8 39.1 %psum.14 = f32[64]{0:T(128)S(1)} all-reduce(f32[64]{0:T(128)S(1)} %multiply_reduce_fusion), channel_id=1, replica_groups=mesh['px'=8,'py'=4] {'px','py'}, use_global_device_ids=true, to_apply=%region_3.0 | all-reduce | flops 64 | bytes 512 | tf_op jit(solution)/shard_map/psum | solution.py:46
  166.7 41.6 %psum.15 = f32[64,64]{1,0:T(8,128)S(1)} all-reduce(f32[64,64]{1,0:T(8,128)S(1)} %convolution_bitcast_fusion.2), channel_id=1, replica_groups=mesh['px'=8,'py'=4] {'px','py'}, use_global_device_ids=true, to_apply=%region_4.0 | all-reduce | flops 4096 | bytes 32768 | tf_op jit(solution)/shard_map/psum | solution.py:50
  (281 shorter events, 69.3 us)
Async XLA Ops:
  3.4 12.6 %collective-permute-start.4 = (bf16[2,64,128]{2,1,0:T(8,128)(2,1)S(1)}, bf16[2,64,128]{2,1,0:T(8,128)(2,1)S(1)}, u32[]{:S(2)}, u32[]{:S(2)}) collective-permute-start(bf16[2,64,128]{2,1,0:T(8,128)(2,1)S(1)} %get-tuple-element.65), channel_id=1, source_target_pairs={{0,4},{4,8},{8,12},{12,16},{16,20},{20,24},{24,28},{28,0},{1,5},{5... | collective-permute-start | bytes 98312 | tf_op jit(solution)/shard_map/ppermute | solution.py:12
  3.9 12.1 %collective-permute-start.6 = (bf16[2,64,128]{2,1,0:T(8,128)(2,1)S(1)}, bf16[2,64,128]{2,1,0:T(8,128)(2,1)S(1)}, u32[]{:S(2)}, u32[]{:S(2)}) collective-permute-start(bf16[2,64,128]{2,1,0:T(8,128)(2,1)S(1)} %get-tuple-element.66), channel_id=1, source_target_pairs={{0,1},{1,2},{2,3},{3,0},{4,5},{5,6},{6,7},{7,4},{8,9},{9,10},{10,1... | collective-permute-start | bytes 98312 | tf_op jit(solution)/shard_map/ppermute | solution.py:12
  6.5 9.4 %collective-permute-start.5 = (bf16[2,64,128]{2,1,0:T(8,128)(2,1)S(1)}, bf16[2,64,128]{2,1,0:T(8,128)(2,1)S(1)}, u32[]{:S(2)}, u32[]{:S(2)}) collective-permute-start(bf16[2,64,128]{2,1,0:T(8,128)(2,1)S(1)} %get-tuple-element.67), channel_id=1, source_target_pairs={{0,28},{4,0},{8,4},{12,8},{16,12},{20,16},{24,20},{28,24},{1,29},{... | collective-permute-start | bytes 98312 | tf_op jit(solution)/shard_map/ppermute | solution.py:12
  8.8 7.2 %collective-permute-start.7 = (bf16[2,64,128]{2,1,0:T(8,128)(2,1)S(1)}, bf16[2,64,128]{2,1,0:T(8,128)(2,1)S(1)}, u32[]{:S(2)}, u32[]{:S(2)}) collective-permute-start(bf16[2,64,128]{2,1,0:T(8,128)(2,1)S(1)} %get-tuple-element.68), channel_id=1, source_target_pairs={{0,3},{1,0},{2,1},{3,2},{4,7},{5,4},{6,5},{7,6},{8,11},{9,8},{10,9... | collective-permute-start | bytes 98312 | tf_op jit(solution)/shard_map/ppermute | solution.py:12
  19.0 6.0 %collective-permute-start = (bf16[2,64,128]{2,1,0:T(8,128)(2,1)S(1)}, bf16[2,64,128]{2,1,0:T(8,128)(2,1)S(1)}, u32[]{:S(2)}, u32[]{:S(2)}) collective-permute-start(bf16[2,64,128]{2,1,0:T(8,128)(2,1)S(1)} %get-tuple-element.122), channel_id=1, source_target_pairs={{0,3},{1,0},{2,1},{3,2},{4,7},{5,4},{6,5},{7,6},{8,11},{9,8},{10,9... | collective-permute-start | bytes 98312 | tf_op jit(solution)/shard_map/while/body/eval_jaxpr/ppermute | solution.py:12
  20.8 5.7 %collective-permute-start.1 = (bf16[2,64,128]{2,1,0:T(8,128)(2,1)S(1)}, bf16[2,64,128]{2,1,0:T(8,128)(2,1)S(1)}, u32[]{:S(2)}, u32[]{:S(2)}) collective-permute-start(bf16[2,64,128]{2,1,0:T(8,128)(2,1)S(1)} %get-tuple-element.123), channel_id=1, source_target_pairs={{0,1},{1,2},{2,3},{3,0},{4,5},{5,6},{6,7},{7,4},{8,9},{9,10},{10,1... | collective-permute-start | bytes 98312 | tf_op jit(solution)/shard_map/while/body/eval_jaxpr/ppermute | solution.py:12
  31.1 7.4 %collective-permute-start = (bf16[2,64,128]{2,1,0:T(8,128)(2,1)S(1)}, bf16[2,64,128]{2,1,0:T(8,128)(2,1)S(1)}, u32[]{:S(2)}, u32[]{:S(2)}) collective-permute-start(bf16[2,64,128]{2,1,0:T(8,128)(2,1)S(1)} %get-tuple-element.122), channel_id=1, source_target_pairs={{0,3},{1,0},{2,1},{3,2},{4,7},{5,4},{6,5},{7,6},{8,11},{9,8},{10,9... | collective-permute-start | bytes 98312 | tf_op jit(solution)/shard_map/while/body/eval_jaxpr/ppermute | solution.py:12
  33.5 5.7 %collective-permute-start.1 = (bf16[2,64,128]{2,1,0:T(8,128)(2,1)S(1)}, bf16[2,64,128]{2,1,0:T(8,128)(2,1)S(1)}, u32[]{:S(2)}, u32[]{:S(2)}) collective-permute-start(bf16[2,64,128]{2,1,0:T(8,128)(2,1)S(1)} %get-tuple-element.123), channel_id=1, source_target_pairs={{0,1},{1,2},{2,3},{3,0},{4,5},{5,6},{6,7},{7,4},{8,9},{9,10},{10,1... | collective-permute-start | bytes 98312 | tf_op jit(solution)/shard_map/while/body/eval_jaxpr/ppermute | solution.py:12
  33.5 5.7 %collective-permute-start.2 = (bf16[2,64,128]{2,1,0:T(8,128)(2,1)S(1)}, bf16[2,64,128]{2,1,0:T(8,128)(2,1)S(1)}, u32[]{:S(2)}, u32[]{:S(2)}) collective-permute-start(bf16[2,64,128]{2,1,0:T(8,128)(2,1)S(1)} %get-tuple-element.124), channel_id=1, source_target_pairs={{0,28},{4,0},{8,4},{12,8},{16,12},{20,16},{24,20},{28,24},{1,29},{... | collective-permute-start | bytes 98312 | tf_op jit(solution)/shard_map/while/body/eval_jaxpr/ppermute | solution.py:12
  43.8 8.6 %collective-permute-start = (bf16[2,64,128]{2,1,0:T(8,128)(2,1)S(1)}, bf16[2,64,128]{2,1,0:T(8,128)(2,1)S(1)}, u32[]{:S(2)}, u32[]{:S(2)}) collective-permute-start(bf16[2,64,128]{2,1,0:T(8,128)(2,1)S(1)} %get-tuple-element.122), channel_id=1, source_target_pairs={{0,3},{1,0},{2,1},{3,2},{4,7},{5,4},{6,5},{7,6},{8,11},{9,8},{10,9... | collective-permute-start | bytes 98312 | tf_op jit(solution)/shard_map/while/body/eval_jaxpr/ppermute | solution.py:12
  47.4 5.7 %collective-permute-start.1 = (bf16[2,64,128]{2,1,0:T(8,128)(2,1)S(1)}, bf16[2,64,128]{2,1,0:T(8,128)(2,1)S(1)}, u32[]{:S(2)}, u32[]{:S(2)}) collective-permute-start(bf16[2,64,128]{2,1,0:T(8,128)(2,1)S(1)} %get-tuple-element.123), channel_id=1, source_target_pairs={{0,1},{1,2},{2,3},{3,0},{4,5},{5,6},{6,7},{7,4},{8,9},{9,10},{10,1... | collective-permute-start | bytes 98312 | tf_op jit(solution)/shard_map/while/body/eval_jaxpr/ppermute | solution.py:12
  47.4 5.7 %collective-permute-start.2 = (bf16[2,64,128]{2,1,0:T(8,128)(2,1)S(1)}, bf16[2,64,128]{2,1,0:T(8,128)(2,1)S(1)}, u32[]{:S(2)}, u32[]{:S(2)}) collective-permute-start(bf16[2,64,128]{2,1,0:T(8,128)(2,1)S(1)} %get-tuple-element.124), channel_id=1, source_target_pairs={{0,28},{4,0},{8,4},{12,8},{16,12},{20,16},{24,20},{28,24},{1,29},{... | collective-permute-start | bytes 98312 | tf_op jit(solution)/shard_map/while/body/eval_jaxpr/ppermute | solution.py:12
  57.8 8.6 %collective-permute-start = (bf16[2,64,128]{2,1,0:T(8,128)(2,1)S(1)}, bf16[2,64,128]{2,1,0:T(8,128)(2,1)S(1)}, u32[]{:S(2)}, u32[]{:S(2)}) collective-permute-start(bf16[2,64,128]{2,1,0:T(8,128)(2,1)S(1)} %get-tuple-element.122), channel_id=1, source_target_pairs={{0,3},{1,0},{2,1},{3,2},{4,7},{5,4},{6,5},{7,6},{8,11},{9,8},{10,9... | collective-permute-start | bytes 98312 | tf_op jit(solution)/shard_map/while/body/eval_jaxpr/ppermute | solution.py:12
  61.4 5.7 %collective-permute-start.1 = (bf16[2,64,128]{2,1,0:T(8,128)(2,1)S(1)}, bf16[2,64,128]{2,1,0:T(8,128)(2,1)S(1)}, u32[]{:S(2)}, u32[]{:S(2)}) collective-permute-start(bf16[2,64,128]{2,1,0:T(8,128)(2,1)S(1)} %get-tuple-element.123), channel_id=1, source_target_pairs={{0,1},{1,2},{2,3},{3,0},{4,5},{5,6},{6,7},{7,4},{8,9},{9,10},{10,1... | collective-permute-start | bytes 98312 | tf_op jit(solution)/shard_map/while/body/eval_jaxpr/ppermute | solution.py:12
  61.4 5.7 %collective-permute-start.2 = (bf16[2,64,128]{2,1,0:T(8,128)(2,1)S(1)}, bf16[2,64,128]{2,1,0:T(8,128)(2,1)S(1)}, u32[]{:S(2)}, u32[]{:S(2)}) collective-permute-start(bf16[2,64,128]{2,1,0:T(8,128)(2,1)S(1)} %get-tuple-element.124), channel_id=1, source_target_pairs={{0,28},{4,0},{8,4},{12,8},{16,12},{20,16},{24,20},{28,24},{1,29},{... | collective-permute-start | bytes 98312 | tf_op jit(solution)/shard_map/while/body/eval_jaxpr/ppermute | solution.py:12
  71.7 8.6 %collective-permute-start = (bf16[2,64,128]{2,1,0:T(8,128)(2,1)S(1)}, bf16[2,64,128]{2,1,0:T(8,128)(2,1)S(1)}, u32[]{:S(2)}, u32[]{:S(2)}) collective-permute-start(bf16[2,64,128]{2,1,0:T(8,128)(2,1)S(1)} %get-tuple-element.122), channel_id=1, source_target_pairs={{0,3},{1,0},{2,1},{3,2},{4,7},{5,4},{6,5},{7,6},{8,11},{9,8},{10,9... | collective-permute-start | bytes 98312 | tf_op jit(solution)/shard_map/while/body/eval_jaxpr/ppermute | solution.py:12
  75.3 5.7 %collective-permute-start.1 = (bf16[2,64,128]{2,1,0:T(8,128)(2,1)S(1)}, bf16[2,64,128]{2,1,0:T(8,128)(2,1)S(1)}, u32[]{:S(2)}, u32[]{:S(2)}) collective-permute-start(bf16[2,64,128]{2,1,0:T(8,128)(2,1)S(1)} %get-tuple-element.123), channel_id=1, source_target_pairs={{0,1},{1,2},{2,3},{3,0},{4,5},{5,6},{6,7},{7,4},{8,9},{9,10},{10,1... | collective-permute-start | bytes 98312 | tf_op jit(solution)/shard_map/while/body/eval_jaxpr/ppermute | solution.py:12
  75.3 5.7 %collective-permute-start.2 = (bf16[2,64,128]{2,1,0:T(8,128)(2,1)S(1)}, bf16[2,64,128]{2,1,0:T(8,128)(2,1)S(1)}, u32[]{:S(2)}, u32[]{:S(2)}) collective-permute-start(bf16[2,64,128]{2,1,0:T(8,128)(2,1)S(1)} %get-tuple-element.124), channel_id=1, source_target_pairs={{0,28},{4,0},{8,4},{12,8},{16,12},{20,16},{24,20},{28,24},{1,29},{... | collective-permute-start | bytes 98312 | tf_op jit(solution)/shard_map/while/body/eval_jaxpr/ppermute | solution.py:12
  85.7 8.6 %collective-permute-start = (bf16[2,64,128]{2,1,0:T(8,128)(2,1)S(1)}, bf16[2,64,128]{2,1,0:T(8,128)(2,1)S(1)}, u32[]{:S(2)}, u32[]{:S(2)}) collective-permute-start(bf16[2,64,128]{2,1,0:T(8,128)(2,1)S(1)} %get-tuple-element.122), channel_id=1, source_target_pairs={{0,3},{1,0},{2,1},{3,2},{4,7},{5,4},{6,5},{7,6},{8,11},{9,8},{10,9... | collective-permute-start | bytes 98312 | tf_op jit(solution)/shard_map/while/body/eval_jaxpr/ppermute | solution.py:12
  89.3 5.7 %collective-permute-start.1 = (bf16[2,64,128]{2,1,0:T(8,128)(2,1)S(1)}, bf16[2,64,128]{2,1,0:T(8,128)(2,1)S(1)}, u32[]{:S(2)}, u32[]{:S(2)}) collective-permute-start(bf16[2,64,128]{2,1,0:T(8,128)(2,1)S(1)} %get-tuple-element.123), channel_id=1, source_target_pairs={{0,1},{1,2},{2,3},{3,0},{4,5},{5,6},{6,7},{7,4},{8,9},{9,10},{10,1... | collective-permute-start | bytes 98312 | tf_op jit(solution)/shard_map/while/body/eval_jaxpr/ppermute | solution.py:12
  99.6 8.6 %collective-permute-start = (bf16[2,64,128]{2,1,0:T(8,128)(2,1)S(1)}, bf16[2,64,128]{2,1,0:T(8,128)(2,1)S(1)}, u32[]{:S(2)}, u32[]{:S(2)}) collective-permute-start(bf16[2,64,128]{2,1,0:T(8,128)(2,1)S(1)} %get-tuple-element.122), channel_id=1, source_target_pairs={{0,3},{1,0},{2,1},{3,2},{4,7},{5,4},{6,5},{7,6},{8,11},{9,8},{10,9... | collective-permute-start | bytes 98312 | tf_op jit(solution)/shard_map/while/body/eval_jaxpr/ppermute | solution.py:12
  113.6 8.6 %collective-permute-start = (bf16[2,64,128]{2,1,0:T(8,128)(2,1)S(1)}, bf16[2,64,128]{2,1,0:T(8,128)(2,1)S(1)}, u32[]{:S(2)}, u32[]{:S(2)}) collective-permute-start(bf16[2,64,128]{2,1,0:T(8,128)(2,1)S(1)} %get-tuple-element.122), channel_id=1, source_target_pairs={{0,3},{1,0},{2,1},{3,2},{4,7},{5,4},{6,5},{7,6},{8,11},{9,8},{10,9... | collective-permute-start | bytes 98312 | tf_op jit(solution)/shard_map/while/body/eval_jaxpr/ppermute | solution.py:12
  117.2 5.7 %collective-permute-start.1 = (bf16[2,64,128]{2,1,0:T(8,128)(2,1)S(1)}, bf16[2,64,128]{2,1,0:T(8,128)(2,1)S(1)}, u32[]{:S(2)}, u32[]{:S(2)}) collective-permute-start(bf16[2,64,128]{2,1,0:T(8,128)(2,1)S(1)} %get-tuple-element.123), channel_id=1, source_target_pairs={{0,1},{1,2},{2,3},{3,0},{4,5},{5,6},{6,7},{7,4},{8,9},{9,10},{10,1... | collective-permute-start | bytes 98312 | tf_op jit(solution)/shard_map/while/body/eval_jaxpr/ppermute | solution.py:12
  117.2 5.7 %collective-permute-start.2 = (bf16[2,64,128]{2,1,0:T(8,128)(2,1)S(1)}, bf16[2,64,128]{2,1,0:T(8,128)(2,1)S(1)}, u32[]{:S(2)}, u32[]{:S(2)}) collective-permute-start(bf16[2,64,128]{2,1,0:T(8,128)(2,1)S(1)} %get-tuple-element.124), channel_id=1, source_target_pairs={{0,28},{4,0},{8,4},{12,8},{16,12},{20,16},{24,20},{28,24},{1,29},{... | collective-permute-start | bytes 98312 | tf_op jit(solution)/shard_map/while/body/eval_jaxpr/ppermute | solution.py:12
  (35 other events, 185.2 us)
where the time goes:
time: 210 us; the launch traced here: 209 us
  blocking collectives  80.7 us (38%)
  starting transfers between devices  45.3 us (22%)
  matrix products  38.8 us (18%)
  local copies, waits for them, and re-layouts  32.5 us (15%)
  waiting for transfers between devices  7.41 us (4%)
  other arithmetic  2.36 us (1%)
    ppermute x36, starting transfers between devices, from_behind(): return lax.ppermute(value, axis, pairs)  45.3 us
    psum x1, blocking collectives, shards(): gram_matrix = lax.psum(partial_gram, ('px', 'py')) / total_rows  41.6 us
    psum x1, blocking collectives, shards(): squares = lax.psum(jnp.sum(current * current, axis=(0, 2)), ('px', 'py'))  39.1 us
    dot_general x9, matrix products, operator_apply(): jnp.einsum('rtkj,rtij->rki', gathered, local_tiles, preferred_element_typ...  22.3 us
    dot_general x9, matrix products, operator_apply(): jnp.einsum('rkj,rij->rki', received[halo_slot], halo_tiles, preferred_ele...  16 us
    while x48, local copies, waits for them, and re-layouts  9.86 us
    gather x9, local copies, waits for them, and re-layouts, operator_apply(): gathered = rounded[local_cols]  7.64 us
    ppermute x36, waiting for transfers between devices, from_behind(): return lax.ppermute(value, axis, pairs)  7.41 us
  transfers between devices with their start and end apart: 36, of which 15 were waited for; matrix products, arithmetic and copies ran while one was open for 15% of the time, Pallas kernels for 0%

commit v1 on v0

v1 whole, which is shorter than its diff:
```python
import functools

import jax
import jax.numpy as jnp
from jax import lax
from jax.experimental import pallas as pl
from jax.experimental.pallas import tpu as pltpu
from jax.sharding import PartitionSpec as P

DEG = 9
MESH = pl.DeviceIdType.MESH
NT = (((1,), (1,)), ((), ()))


def dot_nt(a, b):
    return lax.dot_general(a, b, NT, preferred_element_type=jnp.float32)


def filter_kernel(
    n_px, n_py, cols, slots, bnd, start_hbm, tiles_hbm, halo_hbm, y_hbm, g_out,
    y, vb, acc, tiles, halo, snd, rcv, cur, stk, gx, gy,
    in_sem, out_sem, snd_sem, rcv_sem, gx_snd, gx_rcv, gy_snd, gy_rcv,
):
    rb, tpr = tiles.shape[0], tiles.shape[1]
    nb = bnd.shape[1]
    i, j = lax.axis_index("px"), lax.axis_index("py")
    targets = (
        {"px": lax.rem(i + 1, n_px)},
        {"px": lax.rem(i + n_px - 1, n_px)},
        {"py": lax.rem(j + 1, n_py)},
        {"py": lax.rem(j + n_py - 1, n_py)},
    )

    load_start = pltpu.make_async_copy(start_hbm, y.at[0], in_sem.at[0])
    load_tiles = pltpu.make_async_copy(tiles_hbm, tiles, in_sem.at[1])
    load_halo = pltpu.make_async_copy(halo_hbm, halo, in_sem.at[2])
    load_start.start()
    load_tiles.start()
    load_halo.start()

    barrier = pltpu.get_barrier_semaphore()
    for off in range(1, n_px):
        pl.semaphore_signal(
            barrier, inc=1, device_id={"px": lax.rem(i + off, n_px)}, device_id_type=MESH
        )
    for off in range(1, n_py):
        pl.semaphore_signal(
            barrier, inc=1, device_id={"py": lax.rem(j + off, n_py)}, device_id_type=MESH
        )

    def exchange(step, d):
        rows = pl.ds(d * nb, nb)
        return pltpu.make_async_remote_copy(
            src_ref=snd.at[step, rows],
            dst_ref=rcv.at[step, rows],
            send_sem=snd_sem.at[step, d],
            recv_sem=rcv_sem.at[step, d],
            device_id=targets[d],
            device_id_type=MESH,
        )

    def local_product():
        for r in range(rb):
            gathered = jnp.concatenate([vb[cols[r, t]] for t in range(tpr)], axis=1)
            weights = jnp.concatenate([tiles[r, t] for t in range(tpr)], axis=1)
            acc[r] = dot_nt(gathered, weights)

    load_start.wait()
    vb[...] = y[0].astype(jnp.bfloat16)
    y[1] = jnp.zeros_like(y[1])
    for d in (3, 2, 1, 0):
        for b in range(nb):
            snd[0, d * nb + b] = vb[bnd[d, b]]
    pl.semaphore_wait(barrier, n_px + n_py - 2)
    for d in (3, 2, 1, 0):
        exchange(0, d).start()
    load_tiles.wait()
    load_halo.wait()
    local_product()

    def receive(step):
        for d in range(4):
            exchange(step, d).wait_recv()
        cur[...] = rcv[step]

    def next_rows(row, factor, older):
        coupled = dot_nt(cur[slots[row]], halo[row])
        return factor * (acc[row] + coupled) - y[older, row]

    def advance(step, carry):
        older = lax.rem(step + 1, 2)
        factor = jnp.where(step == 0, 1.0, 2.0).astype(jnp.float32)
        receive(step)
        for d in (3, 2, 1, 0):
            for b in range(nb):
                snd[step + 1, d * nb + b] = next_rows(bnd[d, b], factor, older).astype(jnp.bfloat16)
            exchange(step + 1, d).start()
        for r in range(rb):
            value = next_rows(r, factor, older)
            y[older, r] = value
            vb[r] = value.astype(jnp.bfloat16)
        local_product()
        return carry

    lax.fori_loop(0, DEG - 1, advance, 0)

    last, older = DEG - 1, DEG % 2
    receive(last)
    k, bs = y.shape[2], y.shape[3]
    for r in range(rb):
        value = next_rows(r, 2.0, older)
        y[older, r] = value
        high = value.astype(jnp.bfloat16)
        stk[0:k, r * bs:(r + 1) * bs] = high
        stk[k:2 * k, r * bs:(r + 1) * bs] = (value - high.astype(jnp.float32)).astype(jnp.bfloat16)
    store_y = pltpu.make_async_copy(y.at[older], y_hbm, out_sem)
    store_y.start()
    both = dot_nt(stk[...], stk[...])
    both = both[0:k] + both[k:2 * k]
    raw = both[:, 0:k] + both[:, k:2 * k]
    half = k // 2

    def all_sum(part, buf, axis, here, count, send_sems, recv_sems):
        buf[here] = part
        copies = []
        for off in range(1, count):
            copy = pltpu.make_async_remote_copy(
                src_ref=buf.at[here],
                dst_ref=buf.at[here],
                send_sem=send_sems.at[off],
                recv_sem=recv_sems.at[here],
                device_id={axis: lax.rem(here + off, count)},
                device_id_type=MESH,
            )
            copy.start()
            copies.append(copy)
        for off in range(1, count):
            other = lax.rem(here + off, count)
            pltpu.make_async_remote_copy(
                src_ref=buf.at[other],
                dst_ref=buf.at[other],
                send_sem=send_sems.at[off],
                recv_sem=recv_sems.at[other],
                device_id={axis: other},
                device_id_type=MESH,
            ).wait_recv()
        total = buf[0]
        for other in range(1, count):
            total = total + buf[other]
        return total, copies

    packed = jnp.concatenate([raw[0:half], raw[half:k]], axis=1)
    row_sum, copies_x = all_sum(packed, gx, "px", i, n_px, gx_snd, gx_rcv)
    total, copies_y = all_sum(row_sum, gy, "py", j, n_py, gy_snd, gy_rcv)
    g_out[...] = total

    for copy in copies_x + copies_y:
        copy.wait_send()

    def drain(step, carry):
        for d in range(4):
            exchange(step, d).wait_send()
        return carry

    lax.fori_loop(0, DEG, drain, 0)
    store_y.wait()


def scale_kernel(total_rows, y_ref, g_ref, f_ref, gram_ref):
    half = g_ref.shape[0]
    k = 2 * half
    g = g_ref[...]
    raw = jnp.concatenate([g[:, 0:k], g[:, k:2 * k]], axis=0)
    on_diag = lax.broadcasted_iota(jnp.int32, (k, k), 0) == lax.broadcasted_iota(
        jnp.int32, (k, k), 1
    )
    diag = jnp.where(on_diag, raw, 0.0)
    scale_col = lax.rsqrt(jnp.sum(diag, axis=1, keepdims=True) / total_rows + 1e-06)
    scale_row = lax.rsqrt(jnp.sum(diag, axis=0, keepdims=True) / total_rows + 1e-06)
    gram = raw * scale_col * scale_row / total_rows
    gram_ref[...] = jnp.where((scale_col == 0.0) | (scale_row == 0.0), 0.0, gram)
    f_ref[...] = y_ref[...] * scale_col[None]


def shards(n_px, n_py, start_vecs, local_tiles, local_cols, halo_tiles, halo_slot, boundary):
    rb, k, bs = start_vecs.shape
    nb = boundary.shape[1]
    total_rows = rb * bs * n_px * n_py
    f32, bf16 = jnp.float32, jnp.bfloat16
    smem = pl.BlockSpec(memory_space=pltpu.SMEM)
    vmem = pl.BlockSpec(memory_space=pltpu.VMEM)
    anywhere = pl.BlockSpec(memory_space=pl.ANY)
    dma = pltpu.SemaphoreType.DMA
    flops = 2 * DEG * rb * (local_cols.shape[1] + 1) * k * bs * bs
    vecs, gram_sum = pl.pallas_call(
        functools.partial(filter_kernel, n_px, n_py),
        out_shape=(
            jax.ShapeDtypeStruct((rb, k, bs), f32),
            jax.ShapeDtypeStruct((k // 2, 2 * k), f32),
        ),
        in_specs=[smem, smem, smem, anywhere, anywhere, anywhere],
        out_specs=(anywhere, vmem),
        scratch_shapes=[
            pltpu.VMEM((2, rb, k, bs), f32),
            pltpu.VMEM((rb, k, bs), bf16),
            pltpu.VMEM((rb, k, bs), f32),
            pltpu.VMEM(local_tiles.shape, bf16),
            pltpu.VMEM(halo_tiles.shape, bf16),
            pltpu.VMEM((DEG, 4 * nb, k, bs), bf16),
            pltpu.VMEM((DEG, 4 * nb, k, bs), bf16),
            pltpu.VMEM((4 * nb, k, bs), bf16),
            pltpu.VMEM((2 * k, rb * bs), bf16),
            pltpu.VMEM((n_px, k // 2, 2 * k), f32),
            pltpu.VMEM((n_py, k // 2, 2 * k), f32),
            dma((3,)),
            dma,
            dma((DEG, 4)),
            dma((DEG, 4)),
            dma((n_px,)),
            dma((n_px,)),
            dma((n_py,)),
            dma((n_py,)),
        ],
        compiler_params=pltpu.CompilerParams(
            collective_id=0, has_side_effects=True, vmem_limit_bytes=48 * 1024 * 1024
        ),
        cost_estimate=pl.CostEstimate(
            flops=flops, bytes_accessed=4 * 1024 * 1024, transcendentals=0
        ),
    )(local_cols, halo_slot, boundary, start_vecs, local_tiles, halo_tiles)
    return pl.pallas_call(
        functools.partial(scale_kernel, total_rows),
        out_shape=(
            jax.ShapeDtypeStruct((rb, k, bs), f32),
            jax.ShapeDtypeStruct((k, k), f32),
        ),
        in_specs=[vmem, vmem],
        out_specs=(vmem, vmem),
        cost_estimate=pl.CostEstimate(
            flops=rb * k * bs, bytes_accessed=2 * 4 * rb * k * bs, transcendentals=k
        ),
    )(vecs, gram_sum)


def solution(mesh):
    return jax.shard_map(
        functools.partial(shards, mesh.shape["px"], mesh.shape["py"]),
        mesh=mesh,
        in_specs=(
            P(("px", "py"), None, None),
            P(("px", "py"), None, None, None),
            P(("px", "py"), None),
            P(("px", "py"), None, None),
            P(("px", "py")),
            P(("px", "py"), None),
        ),
        out_specs=(P(("px", "py"), None, None), P()),
        check_vma=False,
    )
```

time: 210 us -> 63.6 us (0.30)
  blocking collectives: 80.7 us -> 0 us
  Pallas kernels: 0 us -> 55.4 us
  starting transfers between devices: 45.3 us -> 0 us
  matrix products: 38.8 us -> 0 us
  local copies, waits for them, and re-layouts: 32.5 us -> 7.23 us
  waiting for transfers between devices: 7.41 us -> 0 us
  other arithmetic: 2.36 us -> 0 us
    psum x2 -> x0, blocking collectives: 80.7 us -> none  [the longest x1 41.6 us: shards(): gram_matrix = lax.psum(partial_gram, ('px', 'py')) / total_rows]
    pallas_call x0 -> x2, Pallas kernels: none -> 55.4 us  [the longest x1 53.4 us: shards(): pl.pallas_call(functools.partial(filter_kernel, n_px, n_py), out_shape=(j...]
    ppermute x36 -> x0, starting transfers between devices: 45.3 us -> none  [from_behind(): return lax.ppermute(value, axis, pairs)]
    dot_general x19 -> x0, matrix products: 38.8 us -> none  [the longest x9 22.3 us: operator_apply(): jnp.einsum('rtkj,rtij->rki', gathered, local_tiles, preferred_element_typ...]
    gather x27 -> x0, local copies, waits for them, and re-layouts: 18.2 us -> none  [the longest x9 7.64 us: operator_apply(): gathered = rounded[local_cols]]
    while x48 -> x0, local copies, waits for them, and re-layouts: 9.86 us -> none
    ppermute x36 -> x0, waiting for transfers between devices: 7.41 us -> none  [from_behind(): return lax.ppermute(value, axis, pairs)]
    unnamed x15 -> x14, local copies, waits for them, and re-layouts: 1.23 us -> 7.23 us
  transfers between devices with their start and end apart: 36 -> 0, of which waited for: 15 -> 0; matrix products, arithmetic and copies ran while one was open for 15% -> 0% of each run, Pallas kernels for 0% -> 0%
where the time goes in v1:
time: 63.6 us; the launch traced here: 63.3 us
  Pallas kernels  55.4 us (87%)
  local copies, waits for them, and re-layouts  7.23 us (11%)
  between operations  0.65 us (1%)
    pallas_call x1, Pallas kernels, shards(): pl.pallas_call(functools.partial(filter_kernel, n_px, n_py), out_shape=(j...  53.4 us
    unnamed x14, local copies, waits for them, and re-layouts  7.23 us
    pallas_call x1, Pallas kernels, shards(): pl.pallas_call(functools.partial(scale_kernel, total_rows), out_shape=(ja...  2.02 us

profile of v1, /device:TPU:0, one launch (start us, length us, event | category | flops | bytes accessed | tf_op | source)
XLA Modules:
  0.0 63.3 jit_solution(5393008280444664842)
XLA Ops:
  0.6 0.8 %copy.9.bnd = s32[4,2]{1,0:T(4,128)S(1)} copy(s32[4,2]{0,1:T(2,128)} %param.11) | data formatting | bytes 64 | tf_op args[5]
  1.4 0.8 %copy.8.cols = s32[16,4]{1,0:T(8,128)S(1)} copy(s32[16,4]{0,1:T(4,128)} %param.8) | data formatting | bytes 512 | tf_op args[2]
  2.2 0.0 copy-start.2
  2.2 1.6 %copy-done.2 = bf16[16,4,128,128]{3,2,1,0:T(8,128)(2,1)S(1)} copy-done((bf16[16,4,128,128]{3,2,1,0:T(8,128)(2,1)S(1)}, bf16[16,4,128,128]{3,2,1,0:T(8,128)(2,1)}, u32[]{:S(2)}) %copy-start.2) | copy-done | bytes 2097176
  3.7 0.0 copy-start.3
  3.7 1.0 %copy-done.3 = f32[16,64,128]{2,1,0:T(8,128)S(1)} copy-done((f32[16,64,128]{2,1,0:T(8,128)S(1)}, f32[16,64,128]{2,1,0:T(8,128)}, u32[]{:S(2)}) %copy-start.3) | copy-done | bytes 524312
  4.8 0.0 copy-start.4
  4.8 1.0 %copy-done.4 = bf16[16,128,128]{2,1,0:T(8,128)(2,1)S(1)} copy-done((bf16[16,128,128]{2,1,0:T(8,128)(2,1)S(1)}, bf16[16,128,128]{2,1,0:T(8,128)(2,1)}, u32[]{:S(2)}) %copy-start.4) | copy-done | bytes 524312
  5.8 0.0 copy-start.5
  5.8 0.7 %copy-done.5 = s32[16]{0:T(128)S(1)} copy-done((s32[16]{0:T(128)S(1)}, s32[16]{0:T(128)}, u32[]{:S(2)}) %copy-start.5) | copy-done | bytes 88
  6.5 53.4 %shard_map.77 = (f32[16,64,128]{2,1,0:T(8,128)S(1)}, f32[32,128]{1,0:T(8,128)S(1)}) custom-call(s32[16,4]{1,0:T(8,128)S(1)} %copy.8.cols, s32[16]{0:T(128)S(1)} %copy-done.5, s32[4,2]{1,0:T(4,128)S(1)} %copy.9.bnd, f32[16,64,128]{2,1,0:T(8,128)S(1)} %copy-done.3, bf16[16,4,128,128]{3,2,1,0:T(8,128)(2,1)S(1)} %copy-done.2, bf16[16,128,128]{2,1,0:T(8,128)(2,1)S(1)} %copy-done.4), custom_call_target="tpu_custom_call" | custom-call | flops 1509949440 | bytes 4194304 | tf_op jit(solution)/shard_map/pallas_call | solution.py:195
  59.9 0.0 copy-start
  59.9 0.8 %copy-done = f32[16,64,128]{2,1,0:T(8,128)} copy-done((f32[16,64,128]{2,1,0:T(8,128)}, f32[16,64,128]{2,1,0:T(8,128)S(1)}, u32[]{:S(2)}) %copy-start) | copy-done | bytes 524312
  60.7 0.0 copy-start.1
  60.7 0.6 copy-done.1
  61.3 2.0 %shard_map.78 = (f32[16,64,128]{2,1,0:T(8,128)}, f32[64,64]{1,0:T(8,128)}) custom-call(f32[16,64,128]{2,1,0:T(8,128)} %copy-done, f32[32,128]{1,0:T(8,128)} %copy-done.1), custom_call_target="tpu_custom_call" | custom-call | flops 131072 | bytes 1048576 | tf_op jit(solution)/shard_map/pallas_call | solution.py:231
Async XLA Ops:
  2.2 1.6 %copy-start.2 = (bf16[16,4,128,128]{3,2,1,0:T(8,128)(2,1)S(1)}, bf16[16,4,128,128]{3,2,1,0:T(8,128)(2,1)}, u32[]{:S(2)}) copy-start(bf16[16,4,128,128]{3,2,1,0:T(8,128)(2,1)} %tiles_hbm.1) | copy-start | bytes 6291460
  3.7 1.0 %copy-start.3 = (f32[16,64,128]{2,1,0:T(8,128)S(1)}, f32[16,64,128]{2,1,0:T(8,128)}, u32[]{:S(2)}) copy-start(f32[16,64,128]{2,1,0:T(8,128)} %start_hbm.1) | copy-start | bytes 1572868
  4.8 1.0 %copy-start.4 = (bf16[16,128,128]{2,1,0:T(8,128)(2,1)S(1)}, bf16[16,128,128]{2,1,0:T(8,128)(2,1)}, u32[]{:S(2)}) copy-start(bf16[16,128,128]{2,1,0:T(8,128)(2,1)} %halo_hbm.1) | copy-start | bytes 1572868
  5.8 0.7 %copy-start.5 = (s32[16]{0:T(128)S(1)}, s32[16]{0:T(128)}, u32[]{:S(2)}) copy-start(s32[16]{0:T(128)} %slots.1) | copy-start | bytes 196
  59.9 0.8 %copy-start = (f32[16,64,128]{2,1,0:T(8,128)}, f32[16,64,128]{2,1,0:T(8,128)S(1)}, u32[]{:S(2)}) copy-start(f32[16,64,128]{2,1,0:T(8,128)S(1)} %get-tuple-element.4.y_ref) | copy-start | bytes 1572868
  60.7 0.6 copy-start.1

commit v2 on v1

--- a/solution.py
+++ b/solution.py
@@ -8,6 +8,8 @@
 from jax.sharding import PartitionSpec as P
 
 DEG = 9
+VMEM_BYTES = 64 * 1024 * 1024
+CHUNKS = 4
 MESH = pl.DeviceIdType.MESH
 NT = (((1,), (1,)), ((), ()))
 
@@ -16,13 +18,17 @@
     return lax.dot_general(a, b, NT, preferred_element_type=jnp.float32)
 
 
+def dot(a, b):
+    return jnp.dot(a, b, preferred_element_type=jnp.float32)
+
+
 def filter_kernel(
     n_px, n_py, cols, slots, bnd, start_hbm, tiles_hbm, halo_hbm, y_hbm, g_out,
-    y, vb, acc, tiles, halo, snd, rcv, cur, stk, gx, gy,
+    y, vb, acc, tiles, halo, tiles_t, halo_t, snd, rcv, cur, stk, gx, gy,
     in_sem, out_sem, snd_sem, rcv_sem, gx_snd, gx_rcv, gy_snd, gy_rcv,
 ):
     rb, tpr = tiles.shape[0], tiles.shape[1]
-    nb = bnd.shape[1]
+    nb, bs = bnd.shape[0], tiles.shape[3]
     i, j = lax.axis_index("px"), lax.axis_index("py")
     targets = (
         {"px": lax.rem(i + 1, n_px)},
@@ -61,22 +67,26 @@
 
     def local_product():
         for r in range(rb):
-            gathered = jnp.concatenate([vb[cols[r, t]] for t in range(tpr)], axis=1)
-            weights = jnp.concatenate([tiles[r, t] for t in range(tpr)], axis=1)
-            acc[r] = dot_nt(gathered, weights)
+            gathered = jnp.concatenate([vb[cols[t, r]] for t in range(tpr)], axis=1)
+            acc[r] = dot(gathered, tiles_t[r])
 
     load_start.wait()
     vb[...] = y[0].astype(jnp.bfloat16)
     y[1] = jnp.zeros_like(y[1])
     for d in (3, 2, 1, 0):
         for b in range(nb):
-            snd[0, d * nb + b] = vb[bnd[d, b]]
+            snd[0, d * nb + b] = vb[bnd[b, d]]
     pl.semaphore_wait(barrier, n_px + n_py - 2)
     for d in (3, 2, 1, 0):
         exchange(0, d).start()
     load_tiles.wait()
+    for r in range(rb):
+        for t in range(tpr):
+            tiles_t[r, t * bs:(t + 1) * bs] = tiles[r, t].T
+    local_product()
     load_halo.wait()
-    local_product()
+    for r in range(rb):
+        halo_t[r] = halo[r].T
 
     def receive(step):
         for d in range(4):
@@ -84,7 +94,7 @@
         cur[...] = rcv[step]
 
     def next_rows(row, factor, older):
-        coupled = dot_nt(cur[slots[row]], halo[row])
+        coupled = dot(cur[slots[row]], halo_t[row])
         return factor * (acc[row] + coupled) - y[older, row]
 
     def advance(step, carry):
@@ -93,7 +103,7 @@
         receive(step)
         for d in (3, 2, 1, 0):
             for b in range(nb):
-                snd[step + 1, d * nb + b] = next_rows(bnd[d, b], factor, older).astype(jnp.bfloat16)
+                snd[step + 1, d * nb + b] = next_rows(bnd[b, d], factor, older).astype(jnp.bfloat16)
             exchange(step + 1, d).start()
         for r in range(rb):
             value = next_rows(r, factor, older)
@@ -106,7 +116,7 @@
 
     last, older = DEG - 1, DEG % 2
     receive(last)
-    k, bs = y.shape[2], y.shape[3]
+    k = y.shape[2]
     for r in range(rb):
         value = next_rows(r, 2.0, older)
         y[older, r] = value
@@ -166,7 +176,13 @@
     store_y.wait()
 
 
-def scale_kernel(total_rows, y_ref, g_ref, f_ref, gram_ref):
+def scale_kernel(total_rows, y_hbm, g_ref, f_hbm, gram_ref, y, f, in_sem, out_sem):
+    rows = y.shape[0] // CHUNKS
+    parts = [pl.ds(c * rows, rows) for c in range(CHUNKS)]
+    loads = [pltpu.make_async_copy(y_hbm.at[p], y.at[p], in_sem.at[c]) for c, p in enumerate(parts)]
+    stores = [pltpu.make_async_copy(f.at[p], f_hbm.at[p], out_sem.at[c]) for c, p in enumerate(parts)]
+    for load in loads:
+        load.start()
     half = g_ref.shape[0]
     k = 2 * half
     g = g_ref[...]
@@ -176,10 +192,15 @@
     )
     diag = jnp.where(on_diag, raw, 0.0)
     scale_col = lax.rsqrt(jnp.sum(diag, axis=1, keepdims=True) / total_rows + 1e-06)
+    for c, p in enumerate(parts):
+        loads[c].wait()
+        f[p] = y[p] * scale_col[None]
+        stores[c].start()
     scale_row = lax.rsqrt(jnp.sum(diag, axis=0, keepdims=True) / total_rows + 1e-06)
     gram = raw * scale_col * scale_row / total_rows
     gram_ref[...] = jnp.where((scale_col == 0.0) | (scale_row == 0.0), 0.0, gram)
-    f_ref[...] = y_ref[...] * scale_col[None]
+    for store in stores:
+        store.wait()
 
 
 def shards(n_px, n_py, start_vecs, local_tiles, local_cols, halo_tiles, halo_slot, boundary):
@@ -205,6 +226,8 @@
             pltpu.VMEM((rb, k, bs), bf16),
             pltpu.VMEM((rb, k, bs), f32),
             pltpu.VMEM(local_tiles.shape, bf16),
+            pltpu.VMEM(halo_tiles.shape, bf16),
+            pltpu.VMEM((rb, local_cols.shape[1] * bs, bs), bf16),
             pltpu.VMEM(halo_tiles.shape, bf16),
             pltpu.VMEM((DEG, 4 * nb, k, bs), bf16),
             pltpu.VMEM((DEG, 4 * nb, k, bs), bf16),
@@ -222,20 +245,27 @@
             dma((n_py,)),
         ],
         compiler_params=pltpu.CompilerParams(
-            collective_id=0, has_side_effects=True, vmem_limit_bytes=48 * 1024 * 1024
+            collective_id=0, has_side_effects=True, vmem_limit_bytes=VMEM_BYTES
         ),
         cost_estimate=pl.CostEstimate(
             flops=flops, bytes_accessed=4 * 1024 * 1024, transcendentals=0
         ),
-    )(local_cols, halo_slot, boundary, start_vecs, local_tiles, halo_tiles)
+    )(local_cols.T, halo_slot, boundary.T, start_vecs, local_tiles, halo_tiles)
     return pl.pallas_call(
         functools.partial(scale_kernel, total_rows),
         out_shape=(
             jax.ShapeDtypeStruct((rb, k, bs), f32),
             jax.ShapeDtypeStruct((k, k), f32),
         ),
-        in_specs=[vmem, vmem],
-        out_specs=(vmem, vmem),
+        in_specs=[anywhere, vmem],
+        out_specs=(anywhere, vmem),
+        scratch_shapes=[
+            pltpu.VMEM((rb, k, bs), f32),
+            pltpu.VMEM((rb, k, bs), f32),
+            dma((CHUNKS,)),
+            dma((CHUNKS,)),
+        ],
+        compiler_params=pltpu.CompilerParams(vmem_limit_bytes=VMEM_BYTES),
         cost_estimate=pl.CostEstimate(
             flops=rb * k * bs, bytes_accessed=2 * 4 * rb * k * bs, transcendentals=k
         ),

time: 63.6 us -> 57.4 us (0.903)
  local copies, waits for them, and re-layouts: 7.23 us -> 0 us
  Pallas kernels: 55.4 us -> 56.5 us
    unnamed x14 -> x0, local copies, waits for them, and re-layouts: 7.23 us -> none
    pallas_call x1, Pallas kernels: 2.02 us -> 3.16 us  [shards(): pl.pallas_call(functools.partial(scale_kernel, total_rows), out_shape=(ja...]
where the time goes in v2:
time: 57.4 us; the launch traced here: 57.1 us
  Pallas kernels  56.5 us (98%)
  between operations  0.64 us (1%)
    pallas_call x1, Pallas kernels, shards(): pl.pallas_call(functools.partial(filter_kernel, n_px, n_py), out_shape=(j...  53.3 us
    pallas_call x1, Pallas kernels, shards(): pl.pallas_call(functools.partial(scale_kernel, total_rows), out_shape=(ja...  3.16 us

profile of v2, /device:TPU:0, one launch (start us, length us, event | category | flops | bytes accessed | tf_op | source)
XLA Modules:
  0.0 57.1 jit_solution(3580159507666707518)
XLA Ops:
  0.6 53.3 %shard_map.77 = (f32[16,64,128]{2,1,0:T(8,128)}, f32[32,128]{1,0:T(8,128)}) custom-call(s32[4,16]{1,0:T(4,128)} %bitcast.2, s32[16]{0:T(128)} %slots.1, s32[2,4]{1,0:T(2,128)} %bitcast.3, f32[16,64,128]{2,1,0:T(8,128)} %start_hbm.1, bf16[16,4,128,128]{3,2,1,0:T(8,128)(2,1)} %tiles_hbm.1, bf16[16,128,128]{2,1,0:T(8,128)(2,1)} %halo_hbm.1), custom_call_target="tpu_custom_call" | custom-call | flops 1509949440 | bytes 4194304 | tf_op jit(solution)/shard_map/pallas_call | solution.py:216
  54.0 3.2 %shard_map.78 = (f32[16,64,128]{2,1,0:T(8,128)}, f32[64,64]{1,0:T(8,128)}) custom-call(f32[16,64,128]{2,1,0:T(8,128)} %get-tuple-element.4.y_hbm, f32[32,128]{1,0:T(8,128)} %get-tuple-element.5.g_ref), custom_call_target="tpu_custom_call" | custom-call | flops 131072 | bytes 1048576 | tf_op jit(solution)/shard_map/pallas_call | solution.py:254

commit v3 on v2

--- a/solution.py
+++ b/solution.py
@@ -9,7 +9,7 @@
 
 DEG = 9
 VMEM_BYTES = 64 * 1024 * 1024
-CHUNKS = 4
+LAG = 4
 MESH = pl.DeviceIdType.MESH
 NT = (((1,), (1,)), ((), ()))
 
@@ -23,7 +23,7 @@
 
 
 def filter_kernel(
-    n_px, n_py, cols, slots, bnd, start_hbm, tiles_hbm, halo_hbm, y_hbm, g_out,
+    n_px, n_py, cols, slots, bnd, start_hbm, tiles_hbm, halo_hbm, y_hbm, scale_out, gram_out,
     y, vb, acc, tiles, halo, tiles_t, halo_t, snd, rcv, cur, stk, gx, gy,
     in_sem, out_sem, snd_sem, rcv_sem, gx_snd, gx_rcv, gy_snd, gy_rcv,
 ):
@@ -65,10 +65,24 @@
             device_id_type=MESH,
         )
 
+    def lagged(make, keep):
+        pending = []
+        for r in range(rb):
+            pending.append((r, make(r)))
+            if len(pending) > LAG:
+                keep(*pending.pop(0))
+        for row, value in pending:
+            keep(row, value)
+
     def local_product():
-        for r in range(rb):
+        def make(r):
             gathered = jnp.concatenate([vb[cols[t, r]] for t in range(tpr)], axis=1)
-            acc[r] = dot(gathered, tiles_t[r])
+            return dot(gathered, tiles_t[r])
+
+        def keep(r, value):
+            acc[r] = value
+
+        lagged(make, keep)
 
     load_start.wait()
     vb[...] = y[0].astype(jnp.bfloat16)
@@ -101,14 +115,22 @@
         older = lax.rem(step + 1, 2)
         factor = jnp.where(step == 0, 1.0, 2.0).astype(jnp.float32)
         receive(step)
-        for d in (3, 2, 1, 0):
-            for b in range(nb):
-                snd[step + 1, d * nb + b] = next_rows(bnd[b, d], factor, older).astype(jnp.bfloat16)
-            exchange(step + 1, d).start()
-        for r in range(rb):
-            value = next_rows(r, factor, older)
+        for pair in ((3, 2), (1, 0)):
+            blocks = [
+                next_rows(bnd[b, d], factor, older).astype(jnp.bfloat16)
+                for d in pair for b in range(nb)
+            ]
+            for at, d in enumerate(pair):
+                for b in range(nb):
+                    snd[step + 1, d * nb + b] = blocks[at * nb + b]
+            for d in pair:
+                exchange(step + 1, d).start()
+
+        def keep(r, value):
             y[older, r] = value
             vb[r] = value.astype(jnp.bfloat16)
+
+        lagged(lambda r: next_rows(r, factor, older), keep)
         local_product()
         return carry
 
@@ -117,12 +139,14 @@
     last, older = DEG - 1, DEG % 2
     receive(last)
     k = y.shape[2]
-    for r in range(rb):
-        value = next_rows(r, 2.0, older)
+
+    def keep_last(r, value):
         y[older, r] = value
         high = value.astype(jnp.bfloat16)
         stk[0:k, r * bs:(r + 1) * bs] = high
         stk[k:2 * k, r * bs:(r + 1) * bs] = (value - high.astype(jnp.float32)).astype(jnp.bfloat16)
+
+    lagged(lambda r: next_rows(r, 2.0, older), keep_last)
     store_y = pltpu.make_async_copy(y.at[older], y_hbm, out_sem)
     store_y.start()
     both = dot_nt(stk[...], stk[...])
@@ -162,7 +186,17 @@
     packed = jnp.concatenate([raw[0:half], raw[half:k]], axis=1)
     row_sum, copies_x = all_sum(packed, gx, "px", i, n_px, gx_snd, gx_rcv)
     total, copies_y = all_sum(row_sum, gy, "py", j, n_py, gy_snd, gy_rcv)
-    g_out[...] = total
+    raw = jnp.concatenate([total[:, 0:k], total[:, k:2 * k]], axis=0)
+    on_diag = lax.broadcasted_iota(jnp.int32, (k, k), 0) == lax.broadcasted_iota(
+        jnp.int32, (k, k), 1
+    )
+    diag = jnp.where(on_diag, raw, 0.0)
+    total_rows = rb * bs * n_px * n_py
+    scale_col = lax.rsqrt(jnp.sum(diag, axis=1, keepdims=True) / total_rows + 1e-06)
+    scale_row = lax.rsqrt(jnp.sum(diag, axis=0, keepdims=True) / total_rows + 1e-06)
+    scale_out[...] = jnp.broadcast_to(scale_col, scale_out.shape)
+    gram = raw * scale_col * scale_row / total_rows
+    gram_out[...] = jnp.where((scale_col == 0.0) | (scale_row == 0.0), 0.0, gram)
 
     for copy in copies_x + copies_y:
         copy.wait_send()
@@ -176,51 +210,24 @@
     store_y.wait()
 
 
-def scale_kernel(total_rows, y_hbm, g_ref, f_hbm, gram_ref, y, f, in_sem, out_sem):
-    rows = y.shape[0] // CHUNKS
-    parts = [pl.ds(c * rows, rows) for c in range(CHUNKS)]
-    loads = [pltpu.make_async_copy(y_hbm.at[p], y.at[p], in_sem.at[c]) for c, p in enumerate(parts)]
-    stores = [pltpu.make_async_copy(f.at[p], f_hbm.at[p], out_sem.at[c]) for c, p in enumerate(parts)]
-    for load in loads:
-        load.start()
-    half = g_ref.shape[0]
-    k = 2 * half
-    g = g_ref[...]
-    raw = jnp.concatenate([g[:, 0:k], g[:, k:2 * k]], axis=0)
-    on_diag = lax.broadcasted_iota(jnp.int32, (k, k), 0) == lax.broadcasted_iota(
-        jnp.int32, (k, k), 1
-    )
-    diag = jnp.where(on_diag, raw, 0.0)
-    scale_col = lax.rsqrt(jnp.sum(diag, axis=1, keepdims=True) / total_rows + 1e-06)
-    for c, p in enumerate(parts):
-        loads[c].wait()
-        f[p] = y[p] * scale_col[None]
-        stores[c].start()
-    scale_row = lax.rsqrt(jnp.sum(diag, axis=0, keepdims=True) / total_rows + 1e-06)
-    gram = raw * scale_col * scale_row / total_rows
-    gram_ref[...] = jnp.where((scale_col == 0.0) | (scale_row == 0.0), 0.0, gram)
-    for store in stores:
-        store.wait()
-
-
 def shards(n_px, n_py, start_vecs, local_tiles, local_cols, halo_tiles, halo_slot, boundary):
     rb, k, bs = start_vecs.shape
     nb = boundary.shape[1]
-    total_rows = rb * bs * n_px * n_py
     f32, bf16 = jnp.float32, jnp.bfloat16
     smem = pl.BlockSpec(memory_space=pltpu.SMEM)
     vmem = pl.BlockSpec(memory_space=pltpu.VMEM)
     anywhere = pl.BlockSpec(memory_space=pl.ANY)
     dma = pltpu.SemaphoreType.DMA
     flops = 2 * DEG * rb * (local_cols.shape[1] + 1) * k * bs * bs
-    vecs, gram_sum = pl.pallas_call(
+    vecs, scale, gram = pl.pallas_call(
         functools.partial(filter_kernel, n_px, n_py),
         out_shape=(
             jax.ShapeDtypeStruct((rb, k, bs), f32),
-            jax.ShapeDtypeStruct((k // 2, 2 * k), f32),
+            jax.ShapeDtypeStruct((k, bs), f32),
+            jax.ShapeDtypeStruct((k, k), f32),
         ),
         in_specs=[smem, smem, smem, anywhere, anywhere, anywhere],
-        out_specs=(anywhere, vmem),
+        out_specs=(anywhere, vmem, vmem),
         scratch_shapes=[
             pltpu.VMEM((2, rb, k, bs), f32),
             pltpu.VMEM((rb, k, bs), bf16),
@@ -251,25 +258,7 @@
             flops=flops, bytes_accessed=4 * 1024 * 1024, transcendentals=0
         ),
     )(local_cols.T, halo_slot, boundary.T, start_vecs, local_tiles, halo_tiles)
-    return pl.pallas_call(
-        functools.partial(scale_kernel, total_rows),
-        out_shape=(
-            jax.ShapeDtypeStruct((rb, k, bs), f32),
-            jax.ShapeDtypeStruct((k, k), f32),
-        ),
-        in_specs=[anywhere, vmem],
-        out_specs=(anywhere, vmem),
-        scratch_shapes=[
-            pltpu.VMEM((rb, k, bs), f32),
-            pltpu.VMEM((rb, k, bs), f32),
-            dma((CHUNKS,)),
-            dma((CHUNKS,)),
-        ],
-        compiler_params=pltpu.CompilerParams(vmem_limit_bytes=VMEM_BYTES),
-        cost_estimate=pl.CostEstimate(
-            flops=rb * k * bs, bytes_accessed=2 * 4 * rb * k * bs, transcendentals=k
-        ),
-    )(vecs, gram_sum)
+    return vecs * scale[None], gram
 
 
 def solution(mesh):

time: 57.4 us -> 57.7 us (level)
  Pallas kernels: 56.5 us -> 53.6 us
  other arithmetic: 0 us -> 1.88 us
  local copies, waits for them, and re-layouts: 0 us -> 1.37 us
    pallas_call x1 -> x0, Pallas kernels: 3.16 us -> none  [shards(): pl.pallas_call(functools.partial(scale_kernel, total_rows), out_shape=(ja...]
    mul x0 -> x1, other arithmetic: none -> 1.88 us  [shards(): return (vecs * scale[None], gram)]
    unnamed x0 -> x1, local copies, waits for them, and re-layouts: none -> 1.37 us
where the time goes in v3:
time: 57.7 us; the launch traced here: 57.5 us
  Pallas kernels  53.6 us (93%)
  other arithmetic  1.88 us (3%)
  local copies, waits for them, and re-layouts  1.37 us (2%)
  between operations  0.64 us (1%)
    pallas_call x1, Pallas kernels, shards(): pl.pallas_call(functools.partial(filter_kernel, n_px, n_py), out_shape=(j...  53.6 us
    mul x1, other arithmetic, shards(): return (vecs * scale[None], gram)  1.88 us
    unnamed x1, local copies, waits for them, and re-layouts  1.37 us

profile of v3, /device:TPU:0, one launch (start us, length us, event | category | flops | bytes accessed | tf_op | source)
XLA Modules:
  0.0 57.5 jit_solution(14455707925547180595)
XLA Ops:
  0.6 53.6 %shard_map.77 = (f32[16,64,128]{2,1,0:T(8,128)}, f32[64,128]{1,0:T(8,128)}, f32[64,64]{1,0:T(8,128)}) custom-call(s32[4,16]{1,0:T(4,128)} %bitcast.2, s32[16]{0:T(128)} %slots.1, s32[2,4]{1,0:T(2,128)} %bitcast.3, f32[16,64,128]{2,1,0:T(8,128)} %start_hbm.1, bf16[16,4,128,128]{3,2,1,0:T(8,128)(2,1)} %tiles_hbm.1, bf16[16,128,128]{2,1,0:T(8,128)(2,1)} %halo_hbm.1), custom_call_target="tpu_custom_call" | custom-call | flops 1509949440 | bytes 4194304 | tf_op jit(solution)/shard_map/pallas_call | solution.py:222
  54.3 1.9 %broadcast_multiply_fusion = f32[16,64,128]{2,1,0:T(8,128)} fusion(f32[16,64,128]{2,1,0:T(8,128)} %get-tuple-element.5, f32[64,128]{1,0:T(8,128)} %get-tuple-element.6), kind=kLoop, calls=%fused_computation | loop fusion | flops 131072 | bytes 1081344 | tf_op jit(solution)/shard_map/mul | solution.py:261
  56.1 1.4 %copy.9 = f32[64,64]{1,0:T(8,128)} copy(f32[64,64]{1,0:T(8,128)} %get-tuple-element.11) | data formatting | bytes 32768

commit v4 on v2

--- a/solution.py
+++ b/solution.py
@@ -9,6 +9,7 @@
 
 DEG = 9
 VMEM_BYTES = 64 * 1024 * 1024
+LAG = 4
 CHUNKS = 4
 MESH = pl.DeviceIdType.MESH
 NT = (((1,), (1,)), ((), ()))
@@ -54,31 +55,56 @@
             barrier, inc=1, device_id={"py": lax.rem(j + off, n_py)}, device_id_type=MESH
         )
 
-    def exchange(step, d):
+    long_way = jnp.where(j == n_py - 1, 2, 3)
+    short_way = 5 - long_way
+    step_py = jnp.where(j == n_py - 1, 1, n_py - 1)
+    py_targets = ({"py": lax.rem(j + step_py, n_py)}, {"py": lax.rem(j + n_py - step_py, n_py)})
+    order = (
+        ((long_way, py_targets[0]),),
+        ((1, targets[1]), (0, targets[0])),
+        ((short_way, py_targets[1]),),
+    )
+
+    def exchange(step, d, target=None):
         rows = pl.ds(d * nb, nb)
         return pltpu.make_async_remote_copy(
             src_ref=snd.at[step, rows],
             dst_ref=rcv.at[step, rows],
             send_sem=snd_sem.at[step, d],
             recv_sem=rcv_sem.at[step, d],
-            device_id=targets[d],
+            device_id=targets[d] if target is None else target,
             device_id_type=MESH,
         )
 
+    def lagged(make, keep):
+        pending = []
+        for r in range(rb):
+            pending.append((r, make(r)))
+            if len(pending) > LAG:
+                keep(*pending.pop(0))
+        for row, value in pending:
+            keep(row, value)
+
     def local_product():
-        for r in range(rb):
+        def make(r):
             gathered = jnp.concatenate([vb[cols[t, r]] for t in range(tpr)], axis=1)
-            acc[r] = dot(gathered, tiles_t[r])
+            return dot(gathered, tiles_t[r])
+
+        def keep(r, value):
+            acc[r] = value
+
+        lagged(make, keep)
 
     load_start.wait()
     vb[...] = y[0].astype(jnp.bfloat16)
     y[1] = jnp.zeros_like(y[1])
-    for d in (3, 2, 1, 0):
+    for d in range(4):
         for b in range(nb):
             snd[0, d * nb + b] = vb[bnd[b, d]]
     pl.semaphore_wait(barrier, n_px + n_py - 2)
-    for d in (3, 2, 1, 0):
-        exchange(0, d).start()
+    for group in order:
+        for d, target in group:
+            exchange(0, d, target).start()
     load_tiles.wait()
     for r in range(rb):
         for t in range(tpr):
@@ -101,14 +127,22 @@
         older = lax.rem(step + 1, 2)
         factor = jnp.where(step == 0, 1.0, 2.0).astype(jnp.float32)
         receive(step)
-        for d in (3, 2, 1, 0):
-            for b in range(nb):
-                snd[step + 1, d * nb + b] = next_rows(bnd[b, d], factor, older).astype(jnp.bfloat16)
-            exchange(step + 1, d).start()
-        for r in range(rb):
-            value = next_rows(r, factor, older)
+        for group in order:
+            blocks = [
+                next_rows(bnd[b, d], factor, older).astype(jnp.bfloat16)
+                for d, _ in group for b in range(nb)
+            ]
+            for at, (d, _) in enumerate(group):
+                for b in range(nb):
+                    snd[step + 1, d * nb + b] = blocks[at * nb + b]
+            for d, target in group:
+                exchange(step + 1, d, target).start()
+
+        def keep(r, value):
             y[older, r] = value
             vb[r] = value.astype(jnp.bfloat16)
+
+        lagged(lambda r: next_rows(r, factor, older), keep)
         local_product()
         return carry
 
@@ -117,12 +151,14 @@
     last, older = DEG - 1, DEG % 2
     receive(last)
     k = y.shape[2]
-    for r in range(rb):
-        value = next_rows(r, 2.0, older)
+
+    def keep_last(r, value):
         y[older, r] = value
         high = value.astype(jnp.bfloat16)
         stk[0:k, r * bs:(r + 1) * bs] = high
         stk[k:2 * k, r * bs:(r + 1) * bs] = (value - high.astype(jnp.float32)).astype(jnp.bfloat16)
+
+    lagged(lambda r: next_rows(r, 2.0, older), keep_last)
     store_y = pltpu.make_async_copy(y.at[older], y_hbm, out_sem)
     store_y.start()
     both = dot_nt(stk[...], stk[...])
@@ -176,13 +212,17 @@
     store_y.wait()
 
 
-def scale_kernel(total_rows, y_hbm, g_ref, f_hbm, gram_ref, y, f, in_sem, out_sem):
+def scale_kernel(total_rows, y_hbm, g_hbm, f_hbm, gram_hbm, y, f, g_ref, gram_ref, in_sem, out_sem):
     rows = y.shape[0] // CHUNKS
     parts = [pl.ds(c * rows, rows) for c in range(CHUNKS)]
     loads = [pltpu.make_async_copy(y_hbm.at[p], y.at[p], in_sem.at[c]) for c, p in enumerate(parts)]
     stores = [pltpu.make_async_copy(f.at[p], f_hbm.at[p], out_sem.at[c]) for c, p in enumerate(parts)]
+    load_g = pltpu.make_async_copy(g_hbm, g_ref, in_sem.at[CHUNKS])
+    store_g = pltpu.make_async_copy(gram_ref, gram_hbm, out_sem.at[CHUNKS])
+    load_g.start()
     for load in loads:
         load.start()
+    load_g.wait()
     half = g_ref.shape[0]
     k = 2 * half
     g = g_ref[...]
@@ -192,15 +232,17 @@
     )
     diag = jnp.where(on_diag, raw, 0.0)
     scale_col = lax.rsqrt(jnp.sum(diag, axis=1, keepdims=True) / total_rows + 1e-06)
+    scale_row = lax.rsqrt(jnp.sum(diag, axis=0, keepdims=True) / total_rows + 1e-06)
+    gram = raw * scale_col * scale_row / total_rows
+    gram_ref[...] = jnp.where((scale_col == 0.0) | (scale_row == 0.0), 0.0, gram)
+    store_g.start()
     for c, p in enumerate(parts):
         loads[c].wait()
         f[p] = y[p] * scale_col[None]
         stores[c].start()
-    scale_row = lax.rsqrt(jnp.sum(diag, axis=0, keepdims=True) / total_rows + 1e-06)
-    gram = raw * scale_col * scale_row / total_rows
-    gram_ref[...] = jnp.where((scale_col == 0.0) | (scale_row == 0.0), 0.0, gram)
     for store in stores:
         store.wait()
+    store_g.wait()
 
 
 def shards(n_px, n_py, start_vecs, local_tiles, local_cols, halo_tiles, halo_slot, boundary):
@@ -257,13 +299,15 @@
             jax.ShapeDtypeStruct((rb, k, bs), f32),
             jax.ShapeDtypeStruct((k, k), f32),
         ),
-        in_specs=[anywhere, vmem],
-        out_specs=(anywhere, vmem),
+        in_specs=[anywhere, anywhere],
+        out_specs=(anywhere, anywhere),
         scratch_shapes=[
             pltpu.VMEM((rb, k, bs), f32),
             pltpu.VMEM((rb, k, bs), f32),
-            dma((CHUNKS,)),
-            dma((CHUNKS,)),
+            pltpu.VMEM((k // 2, 2 * k), f32),
+            pltpu.VMEM((k, k), f32),
+            dma((CHUNKS + 1,)),
+            dma((CHUNKS + 1,)),
         ],
         compiler_params=pltpu.CompilerParams(vmem_limit_bytes=VMEM_BYTES),
         cost_estimate=pl.CostEstimate(

time: 57.4 us -> 54.2 us (0.944)
  Pallas kernels: 56.5 us -> 53.3 us
    pallas_call x1, Pallas kernels: 53.3 us -> 51.4 us  [shards(): pl.pallas_call(functools.partial(filter_kernel, n_px, n_py), out_shape=(j...]
    pallas_call x1, Pallas kernels: 3.16 us -> 1.86 us  [shards(): pl.pallas_call(functools.partial(scale_kernel, total_rows), out_shape=(ja...]
where the time goes in v4:
time: 54.2 us; the launch traced here: 53.9 us
  Pallas kernels  53.3 us (98%)
  between operations  0.64 us (1%)
    pallas_call x1, Pallas kernels, shards(): pl.pallas_call(functools.partial(filter_kernel, n_px, n_py), out_shape=(j...  51.4 us
    pallas_call x1, Pallas kernels, shards(): pl.pallas_call(functools.partial(scale_kernel, total_rows), out_shape=(ja...  1.86 us

profile of v4, /device:TPU:0, one launch (start us, length us, event | category | flops | bytes accessed | tf_op | source)
XLA Modules:
  0.0 53.9 jit_solution(16334211334218894966)
XLA Ops:
  0.6 51.4 %shard_map.77 = (f32[16,64,128]{2,1,0:T(8,128)}, f32[32,128]{1,0:T(8,128)}) custom-call(s32[4,16]{1,0:T(4,128)} %bitcast.2, s32[16]{0:T(128)} %slots.1, s32[2,4]{1,0:T(2,128)} %bitcast.3, f32[16,64,128]{2,1,0:T(8,128)} %start_hbm.1, bf16[16,4,128,128]{3,2,1,0:T(8,128)(2,1)} %tiles_hbm.1, bf16[16,128,128]{2,1,0:T(8,128)(2,1)} %halo_hbm.1), custom_call_target="tpu_custom_call" | custom-call | flops 1509949440 | bytes 4194304 | tf_op jit(solution)/shard_map/pallas_call | solution.py:258
  52.1 1.9 %shard_map.78 = (f32[16,64,128]{2,1,0:T(8,128)}, f32[64,64]{1,0:T(8,128)}) custom-call(f32[16,64,128]{2,1,0:T(8,128)} %get-tuple-element.4.y_hbm, f32[32,128]{1,0:T(8,128)} %get-tuple-element.5.g_hbm), custom_call_target="tpu_custom_call" | custom-call | flops 131072 | bytes 1048576 | tf_op jit(solution)/shard_map/pallas_call | solution.py:296

commit v5 on v4

--- a/solution.py
+++ b/solution.py
@@ -55,9 +55,10 @@
             barrier, inc=1, device_id={"py": lax.rem(j + off, n_py)}, device_id_type=MESH
         )
 
-    long_way = jnp.where(j == n_py - 1, 2, 3)
+    forward_first = (j == n_py - 1) | ((j > 0) & (2 * j < n_py))
+    long_way = jnp.where(forward_first, 2, 3)
     short_way = 5 - long_way
-    step_py = jnp.where(j == n_py - 1, 1, n_py - 1)
+    step_py = jnp.where(forward_first, 1, n_py - 1)
     py_targets = ({"py": lax.rem(j + step_py, n_py)}, {"py": lax.rem(j + n_py - step_py, n_py)})
     order = (
         ((long_way, py_targets[0]),),
@@ -170,12 +171,18 @@
         buf[here] = part
         copies = []
         for off in range(1, count):
+            down, up = count - off, off - 1
+            peer = jnp.where(
+                2 * here < count,
+                down - jnp.where(down <= here, 1, 0),
+                up + jnp.where(up >= here, 1, 0),
+            )
             copy = pltpu.make_async_remote_copy(
                 src_ref=buf.at[here],
                 dst_ref=buf.at[here],
                 send_sem=send_sems.at[off],
                 recv_sem=recv_sems.at[here],
-                device_id={axis: lax.rem(here + off, count)},
+                device_id={axis: peer},
                 device_id_type=MESH,
             )
             copy.start()

time: 54.2 us -> 54.2 us (level)
  no operation moved by 1% of the time
where the time goes in v5:
time: 54.2 us; the launch traced here: 53.9 us
  Pallas kernels  53.3 us (98%)
  between operations  0.64 us (1%)
    pallas_call x1, Pallas kernels, shards(): pl.pallas_call(functools.partial(filter_kernel, n_px, n_py), out_shape=(j...  51.4 us
    pallas_call x1, Pallas kernels, shards(): pl.pallas_call(functools.partial(scale_kernel, total_rows), out_shape=(ja...  1.86 us

profile of v5, /device:TPU:0, one launch (start us, length us, event | category | flops | bytes accessed | tf_op | source)
XLA Modules:
  0.0 53.9 jit_solution(18128703659736165582)
XLA Ops:
  0.6 51.4 %shard_map.77 = (f32[16,64,128]{2,1,0:T(8,128)}, f32[32,128]{1,0:T(8,128)}) custom-call(s32[4,16]{1,0:T(4,128)} %bitcast.2, s32[16]{0:T(128)} %slots.1, s32[2,4]{1,0:T(2,128)} %bitcast.3, f32[16,64,128]{2,1,0:T(8,128)} %start_hbm.1, bf16[16,4,128,128]{3,2,1,0:T(8,128)(2,1)} %tiles_hbm.1, bf16[16,128,128]{2,1,0:T(8,128)(2,1)} %halo_hbm.1), custom_call_target="tpu_custom_call" | custom-call | flops 1509949440 | bytes 4194304 | tf_op jit(solution)/shard_map/pallas_call | solution.py:265
  52.1 1.9 %shard_map.78 = (f32[16,64,128]{2,1,0:T(8,128)}, f32[64,64]{1,0:T(8,128)}) custom-call(f32[16,64,128]{2,1,0:T(8,128)} %get-tuple-element.4.y_hbm, f32[32,128]{1,0:T(8,128)} %get-tuple-element.5.g_hbm), custom_call_target="tpu_custom_call" | custom-call | flops 131072 | bytes 1048576 | tf_op jit(solution)/shard_map/pallas_call | solution.py:303

commit v6 on v5

--- a/solution.py
+++ b/solution.py
@@ -19,13 +19,9 @@
     return lax.dot_general(a, b, NT, preferred_element_type=jnp.float32)
 
 
-def dot(a, b):
-    return jnp.dot(a, b, preferred_element_type=jnp.float32)
-
-
 def filter_kernel(
     n_px, n_py, cols, slots, bnd, start_hbm, tiles_hbm, halo_hbm, y_hbm, g_out,
-    y, vb, acc, tiles, halo, tiles_t, halo_t, snd, rcv, cur, stk, gx, gy,
+    y, vb, acc, tiles, halo, snd, rcv, cur, stk, gx, gy,
     in_sem, out_sem, snd_sem, rcv_sem, gx_snd, gx_rcv, gy_snd, gy_rcv,
 ):
     rb, tpr = tiles.shape[0], tiles.shape[1]
@@ -89,7 +85,8 @@
     def local_product():
         def make(r):
             gathered = jnp.concatenate([vb[cols[t, r]] for t in range(tpr)], axis=1)
-            return dot(gathered, tiles_t[r])
+            weights = jnp.concatenate([tiles[r, t] for t in range(tpr)], axis=1)
+            return dot_nt(gathered, weights)
 
         def keep(r, value):
             acc[r] = value
@@ -97,23 +94,18 @@
         lagged(make, keep)
 
     load_start.wait()
-    vb[...] = y[0].astype(jnp.bfloat16)
-    y[1] = jnp.zeros_like(y[1])
     for d in range(4):
         for b in range(nb):
-            snd[0, d * nb + b] = vb[bnd[b, d]]
+            snd[0, d * nb + b] = y[0, bnd[b, d]].astype(jnp.bfloat16)
     pl.semaphore_wait(barrier, n_px + n_py - 2)
     for group in order:
         for d, target in group:
             exchange(0, d, target).start()
+    vb[...] = y[0].astype(jnp.bfloat16)
+    y[1] = jnp.zeros_like(y[1])
     load_tiles.wait()
-    for r in range(rb):
-        for t in range(tpr):
-            tiles_t[r, t * bs:(t + 1) * bs] = tiles[r, t].T
     local_product()
     load_halo.wait()
-    for r in range(rb):
-        halo_t[r] = halo[r].T
 
     def receive(step):
         for d in range(4):
@@ -121,7 +113,7 @@
         cur[...] = rcv[step]
 
     def next_rows(row, factor, older):
-        coupled = dot(cur[slots[row]], halo_t[row])
+        coupled = dot_nt(cur[slots[row]], halo[row])
         return factor * (acc[row] + coupled) - y[older, row]
 
     def advance(step, carry):
@@ -276,8 +268,6 @@
             pltpu.VMEM((rb, k, bs), f32),
             pltpu.VMEM(local_tiles.shape, bf16),
             pltpu.VMEM(halo_tiles.shape, bf16),
-            pltpu.VMEM((rb, local_cols.shape[1] * bs, bs), bf16),
-            pltpu.VMEM(halo_tiles.shape, bf16),
             pltpu.VMEM((DEG, 4 * nb, k, bs), bf16),
             pltpu.VMEM((DEG, 4 * nb, k, bs), bf16),
             pltpu.VMEM((4 * nb, k, bs), bf16),

time: 54.2 us -> 54.5 us (level)
  no operation moved by 1% of the time
where the time goes in v6:
time: 54.5 us; the launch traced here: 54.3 us
  Pallas kernels  53.6 us (98%)
  between operations  0.64 us (1%)
    pallas_call x1, Pallas kernels, shards(): pl.pallas_call(functools.partial(filter_kernel, n_px, n_py), out_shape=(j...  51.8 us
    pallas_call x1, Pallas kernels, shards(): pl.pallas_call(functools.partial(scale_kernel, total_rows), out_shape=(ja...  1.86 us

profile of v6, /device:TPU:0, one launch (start us, length us, event | category | flops | bytes accessed | tf_op | source)
XLA Modules:
  0.0 54.3 jit_solution(6979583375971069809)
XLA Ops:
  0.6 51.8 %shard_map.77 = (f32[16,64,128]{2,1,0:T(8,128)}, f32[32,128]{1,0:T(8,128)}) custom-call(s32[4,16]{1,0:T(4,128)} %bitcast.2, s32[16]{0:T(128)} %slots.1, s32[2,4]{1,0:T(2,128)} %bitcast.3, f32[16,64,128]{2,1,0:T(8,128)} %start_hbm.1, bf16[16,4,128,128]{3,2,1,0:T(8,128)(2,1)} %tiles_hbm.1, bf16[16,128,128]{2,1,0:T(8,128)(2,1)} %halo_hbm.1), custom_call_target="tpu_custom_call" | custom-call | flops 1509949440 | bytes 4194304 | tf_op jit(solution)/shard_map/pallas_call | solution.py:257
  52.4 1.9 %shard_map.78 = (f32[16,64,128]{2,1,0:T(8,128)}, f32[64,64]{1,0:T(8,128)}) custom-call(f32[16,64,128]{2,1,0:T(8,128)} %get-tuple-element.4.y_hbm, f32[32,128]{1,0:T(8,128)} %get-tuple-element.5.g_hbm), custom_call_target="tpu_custom_call" | custom-call | flops 131072 | bytes 1048576 | tf_op jit(solution)/shard_map/pallas_call | solution.py:293

commit v7 on v5

--- a/solution.py
+++ b/solution.py
@@ -97,15 +97,15 @@
         lagged(make, keep)
 
     load_start.wait()
-    vb[...] = y[0].astype(jnp.bfloat16)
-    y[1] = jnp.zeros_like(y[1])
     for d in range(4):
         for b in range(nb):
-            snd[0, d * nb + b] = vb[bnd[b, d]]
+            snd[0, d * nb + b] = y[0, bnd[b, d]].astype(jnp.bfloat16)
     pl.semaphore_wait(barrier, n_px + n_py - 2)
     for group in order:
         for d, target in group:
             exchange(0, d, target).start()
+    vb[...] = y[0].astype(jnp.bfloat16)
+    y[1] = jnp.zeros_like(y[1])
     load_tiles.wait()
     for r in range(rb):
         for t in range(tpr):

time: 54.2 us -> 54.2 us (level)
  no operation moved by 1% of the time
where the time goes in v7:
time: 54.2 us; the launch traced here: 53.9 us
  Pallas kernels  53.3 us (98%)
  between operations  0.64 us (1%)
    pallas_call x1, Pallas kernels, shards(): pl.pallas_call(functools.partial(filter_kernel, n_px, n_py), out_shape=(j...  51.4 us
    pallas_call x1, Pallas kernels, shards(): pl.pallas_call(functools.partial(scale_kernel, total_rows), out_shape=(ja...  1.86 us

profile of v7, /device:TPU:0, one launch (start us, length us, event | category | flops | bytes accessed | tf_op | source)
XLA Modules:
  0.0 53.9 jit_solution(18004359801578674118)
XLA Ops:
  0.6 51.4 %shard_map.77 = (f32[16,64,128]{2,1,0:T(8,128)}, f32[32,128]{1,0:T(8,128)}) custom-call(s32[4,16]{1,0:T(4,128)} %bitcast.2, s32[16]{0:T(128)} %slots.1, s32[2,4]{1,0:T(2,128)} %bitcast.3, f32[16,64,128]{2,1,0:T(8,128)} %start_hbm.1, bf16[16,4,128,128]{3,2,1,0:T(8,128)(2,1)} %tiles_hbm.1, bf16[16,128,128]{2,1,0:T(8,128)(2,1)} %halo_hbm.1), custom_call_target="tpu_custom_call" | custom-call | flops 1509949440 | bytes 4194304 | tf_op jit(solution)/shard_map/pallas_call | solution.py:265
  52.1 1.9 %shard_map.78 = (f32[16,64,128]{2,1,0:T(8,128)}, f32[64,64]{1,0:T(8,128)}) custom-call(f32[16,64,128]{2,1,0:T(8,128)} %get-tuple-element.4.y_hbm, f32[32,128]{1,0:T(8,128)} %get-tuple-element.5.g_hbm), custom_call_target="tpu_custom_call" | custom-call | flops 131072 | bytes 1048576 | tf_op jit(solution)/shard_map/pallas_call | solution.py:303
